TPU v7x, 128 devices: a whole 4x4x4 slice. The times are simulated.
128 devices in a mesh: grp: 4 (over y_lo, core), tp: 16 (over x, z), ctx: 2 (over y_hi).
Axes of the slice: x: 4, y: 4 (y_hi: 2, y_lo: 2; y = y_hi * 2 + y_lo), z: 4, core: 2. Of those that a mesh axis runs over, the one named last changes fastest.
Arguments:
- layer_input: bfloat16 [4, 2048, 2048], P('grp', 'ctx'), may hold values from -6 to 6
- ln1_gain: bfloat16 [2048], replicated, may hold values from 0.25 to 1.75
- ln1_bias: bfloat16 [2048], replicated, may hold values from -2.5 to 2.5
- qkv_weight: bfloat16 [2048, 3, 2048], P(None, None, 'tp'), may hold values from -0.1875 to 0.1875
- qv_bias: bfloat16 [2, 2048], P(None, 'tp'), may hold values from -3 to 3
- out_weight: bfloat16 [2048, 2048], P('tp'), may hold values from -0.5 to 0.5
- out_bias: bfloat16 [2048], replicated, may hold values from -2.5 to 2.5
- ln2_gain: bfloat16 [2048], replicated, may hold values from 0.25 to 1.75
- ln2_bias: bfloat16 [2048], replicated, may hold values from -2.5 to 2.5
- up_weight: bfloat16 [2048, 8192], P(None, 'tp'), may hold values from -0.125 to 0.125
- up_bias: bfloat16 [8192], P('tp'), may hold values from -3 to 3
- down_weight: bfloat16 [8192, 2048], P('tp'), may hold values from -0.0625 to 0.0625
- down_bias: bfloat16 [2048], replicated, may hold values from -2.5 to 2.5
- cotangent: bfloat16 [4, 2048, 2048], P('grp', 'ctx'), may hold values from -6 to 6
- group_table: int32 [4], replicated, may hold values from 0 to 2, as said below
- group_counts: int32 [3], replicated, may hold values from 1024 to 16384, as said below
- block_order: int32 [4], replicated, may hold values from 0 to 3, as said below
Outputs:
- layer_output: bfloat16 [4, 2048, 2048], P('grp', 'ctx')
- input_grad: float32 [4, 2048, 2048], P('grp', 'ctx')
- ln1_gain_grad: float32 [2048], replicated
- ln1_bias_grad: float32 [2048], replicated
- qkv_weight_grad: float32 [2048, 3, 2048], P(None, None, 'tp')
- qv_bias_grad: float32 [2, 2048], P(None, 'tp')
- out_weight_grad: float32 [2048, 2048], P('tp')
- out_bias_grad: float32 [2048], replicated
- ln2_gain_grad: float32 [2048], replicated
- ln2_bias_grad: float32 [2048], replicated
- up_weight_grad: float32 [2048, 8192], P(None, 'tp')
- up_bias_grad: float32 [8192], P('tp')
- down_weight_grad: float32 [8192, 2048], P('tp')
- down_bias_grad: float32 [2048], replicated
Inputs may be any that keep to these rules, and one draw needn't show every extreme that they name: `group_table`: every script group sits at one group position or more; group 0 sits at exactly two, each other group at one. `group_counts`: the largest count is exactly 16384. `block_order`: A permutation of the 4 blocks; slots 2 c and 2 c + 1 belong to ctx index c, and their two blocks add up to 3.
All inputs are finite; a program needn't handle non-finite values.
Results may differ from a plain program's by a relative error of at most 0.025.
Values may be sent and summed in bfloat16 or wider, within the bound.
No kernel may reach another device: no remote copies, remote signals or barrier semaphores. Data moves between devices by JAX's collectives and lax.ppermute only.
A program may use at most 192 MiB of HBM per device.

v0:
```python
import math

import jax
import jax.numpy as jnp
from jax import lax
from jax.sharding import PartitionSpec as P

HD = 128
GROUPS = 3


def layer_norm(values, gain_vec, bias_vec):
    average = jnp.mean(values, axis=-1, keepdims=True)
    centred = values - average
    variance = jnp.mean(centred * centred, axis=-1, keepdims=True)
    return centred * lax.rsqrt(variance + 1e-05) * gain_vec + bias_vec


def gelu_tanh(values):
    inner = math.sqrt(2.0 / math.pi) * (values + 0.044715 * values * values * values)
    return 0.5 * values * (1.0 + jnp.tanh(inner))


def token_places(block_order, layout_index, block_rows):
    slots = layout_index // block_rows
    column = jnp.arange(block_order.shape[0], dtype=jnp.int32)
    picked = jnp.sum(
        jnp.where(
            slots[:, None] == column[None, :],
            block_order[None, :],
            jnp.zeros_like(block_order)[None, :],
        ),
        axis=1,
    )
    return picked * block_rows + layout_index % block_rows


def position_shares(group_table, group_counts):
    member = (group_table[:, None] == jnp.arange(GROUPS, dtype=jnp.int32)[None, :]).astype(
        jnp.float32
    )
    holders = jnp.sum(member, axis=0)
    counts_float = group_counts.astype(jnp.float32)
    per_group = counts_float / (holders * jnp.sum(counts_float))
    return group_table.shape[0] * jnp.sum(member * per_group[None, :], axis=1)


def per_device(
    layer_input,
    ln1_gain,
    ln1_bias,
    qkv_weight,
    qv_bias,
    out_weight,
    out_bias,
    ln2_gain,
    ln2_bias,
    up_weight,
    up_bias,
    down_weight,
    down_bias,
    cotangent,
    group_table,
    group_counts,
    block_order,
):
    width = layer_input.shape[-1]
    row_count = layer_input.shape[1]
    local_width = qkv_weight.shape[2]
    heads_here = local_width // HD
    block_rows = row_count // 2
    score_scale = 1.0 / math.sqrt(HD)
    fp32 = jnp.float32
    bf16 = jnp.bfloat16
    gain_one = ln1_gain.astype(fp32)
    bias_one = ln1_bias.astype(fp32)
    gain_two = ln2_gain.astype(fp32)
    bias_two = ln2_bias.astype(fp32)
    out_bias_f = out_bias.astype(fp32)
    up_bias_f = up_bias.astype(fp32)
    down_bias_f = down_bias.astype(fp32)
    query_bias = qv_bias[0].astype(fp32).reshape(heads_here, HD)
    value_bias = qv_bias[1].astype(fp32).reshape(heads_here, HD)
    tokens_in = layer_input.reshape(row_count, width).astype(fp32)
    qkv_flat = qkv_weight.reshape(width, 3 * local_width)
    ctx_count = lax.axis_size("ctx")
    own_layout = lax.axis_index("ctx") * row_count + jnp.arange(row_count, dtype=jnp.int32)
    query_places = token_places(block_order, own_layout, block_rows)
    key_places = token_places(
        block_order, jnp.arange(row_count * ctx_count, dtype=jnp.int32), block_rows
    )
    causal = (query_places[:, None] >= key_places[None, :])[None]

    def attend(rows_in):
        normed = layer_norm(rows_in, gain_one, bias_one).astype(bf16)
        mixed = jnp.dot(normed, qkv_flat, preferred_element_type=fp32).reshape(
            row_count, 3, heads_here, HD
        )
        query_rows = (mixed[:, 0] + query_bias).astype(bf16)
        key_rows = mixed[:, 1].astype(bf16)
        value_rows = (mixed[:, 2] + value_bias).astype(bf16)
        keys_all, values_all = (
            lax.all_gather(key_rows, "ctx", axis=0, tiled=True),
            lax.all_gather(value_rows, "ctx", axis=0, tiled=True),
        )
        scores = (
            jnp.einsum("qhd,khd->hqk", query_rows, keys_all, preferred_element_type=fp32)
            * score_scale
        )
        scores = jnp.where(causal, scores, -1e30)
        top_score = jnp.max(scores, axis=-1, keepdims=True)
        expo = jnp.exp(scores - top_score)
        attn_probs = expo / jnp.sum(expo, axis=-1, keepdims=True)
        probs_low = attn_probs.astype(bf16)
        heads_out = jnp.einsum("hqk,khd->qhd", probs_low, values_all, preferred_element_type=fp32)
        heads_low = heads_out.astype(bf16).reshape(row_count, local_width)
        partial_out = jnp.dot(heads_low, out_weight, preferred_element_type=fp32)
        middle = rows_in + lax.psum(partial_out, "tp") + out_bias_f
        normed_two = layer_norm(middle, gain_two, bias_two).astype(bf16)
        return (
            middle,
            normed_two,
            (normed, query_rows, keys_all, values_all, attn_probs, probs_low, heads_low),
        )

    def mlp_front(normed_two):
        hidden = jnp.dot(normed_two, up_weight, preferred_element_type=fp32) + up_bias_f
        active = gelu_tanh(hidden).astype(bf16)
        return (hidden, active)

    middle, normed_two, kept_values = attend(tokens_in)
    hidden, active = mlp_front(normed_two)
    partial_mlp = jnp.dot(active, down_weight, preferred_element_type=fp32)
    output_full = (
        middle + lax.psum(partial_mlp.astype(jnp.bfloat16), "tp").astype(jnp.float32) + down_bias_f
    )
    layer_output = output_full.astype(bf16)
    tokens_used = lax.optimization_barrier((tokens_in, layer_output))[0]
    middle, normed_two, kept_values = attend(tokens_used)
    hidden, active = mlp_front(normed_two)
    normed, query_rows, keys_all, values_all, attn_probs, probs_low, heads_low = kept_values
    shares = position_shares(group_table, group_counts)
    grp_slots = jnp.arange(shares.shape[0], dtype=jnp.int32)
    my_share = jnp.sum(
        jnp.where(grp_slots == lax.axis_index("grp"), shares, jnp.zeros_like(shares))
    )
    grad_out = cotangent.reshape(row_count, width).astype(fp32) * my_share
    grad_low = grad_out.astype(bf16)
    down_bias_grad = jnp.sum(grad_out, axis=0)
    down_weight_grad = jnp.einsum("rf,rd->fd", active, grad_low, preferred_element_type=fp32)
    active_grad = jnp.einsum("rd,fd->rf", grad_low, down_weight, preferred_element_type=fp32)
    gelu_value, gelu_pull = jax.vjp(gelu_tanh, hidden)
    hidden_grad = gelu_pull(active_grad)[0].astype(bf16)
    up_bias_grad = jnp.sum(hidden_grad.astype(fp32), axis=0)
    up_weight_grad = jnp.einsum("rd,rf->df", normed_two, hidden_grad, preferred_element_type=fp32)
    normed_two_grad = lax.psum(
        jnp.einsum("rf,df->rd", hidden_grad, up_weight, preferred_element_type=fp32).astype(
            jnp.bfloat16
        ),
        "tp",
    ).astype(jnp.float32)
    norm_value, norm_pull = jax.vjp(layer_norm, middle, gain_two, bias_two)
    middle_part, ln2_gain_grad, ln2_bias_grad = norm_pull(normed_two_grad)
    middle_grad = grad_out + middle_part
    middle_low = middle_grad.astype(bf16)
    out_bias_grad = jnp.sum(middle_grad, axis=0)
    out_weight_grad = jnp.einsum("rf,rd->fd", heads_low, middle_low, preferred_element_type=fp32)
    head_grad = (
        jnp.einsum("rd,fd->rf", middle_low, out_weight, preferred_element_type=fp32)
        .astype(bf16)
        .reshape(row_count, heads_here, HD)
    )
    prob_grad = jnp.einsum("qhd,khd->hqk", head_grad, values_all, preferred_element_type=fp32)
    values_grad_all = jnp.einsum("hqk,qhd->khd", probs_low, head_grad, preferred_element_type=fp32)
    score_grad = (
        attn_probs * (prob_grad - jnp.sum(attn_probs * prob_grad, axis=-1, keepdims=True))
    ).astype(bf16)
    query_grad = (
        jnp.einsum("hqk,khd->qhd", score_grad, keys_all, preferred_element_type=fp32) * score_scale
    ).astype(bf16)
    keys_grad_all = (
        jnp.einsum("hqk,qhd->khd", score_grad, query_rows, preferred_element_type=fp32)
        * score_scale
    )
    key_grad, value_grad = (
        lax.psum_scatter(
            keys_grad_all.astype(jnp.bfloat16), "ctx", scatter_dimension=0, tiled=True
        ).astype(jnp.float32),
        lax.psum_scatter(
            values_grad_all.astype(jnp.bfloat16), "ctx", scatter_dimension=0, tiled=True
        ).astype(jnp.float32),
    )
    key_low = key_grad.astype(bf16)
    value_low = value_grad.astype(bf16)
    qkv_grad = jnp.stack([query_grad, key_low, value_low], axis=1).reshape(
        row_count, 3 * local_width
    )
    qv_bias_grad = jnp.stack(
        [
            jnp.sum(query_grad.astype(fp32), axis=0).reshape(local_width),
            jnp.sum(value_low.astype(fp32), axis=0).reshape(local_width),
        ]
    )
    qkv_weight_grad = jnp.einsum(
        "rd,rc->dc", normed, qkv_grad, preferred_element_type=fp32
    ).reshape(width, 3, local_width)
    normed_grad = lax.psum(
        jnp.einsum("rc,dc->rd", qkv_grad, qkv_flat, preferred_element_type=fp32).astype(
            jnp.bfloat16
        ),
        "tp",
    ).astype(jnp.float32)
    first_value, first_pull = jax.vjp(layer_norm, tokens_used, gain_one, bias_one)
    input_part, ln1_gain_grad, ln1_bias_grad = first_pull(normed_grad)
    input_grad = middle_grad + input_part
    (
        ln1_gain_grad,
        ln1_bias_grad,
        qkv_weight_grad,
        qv_bias_grad,
        out_weight_grad,
        out_bias_grad,
        ln2_gain_grad,
        ln2_bias_grad,
        up_weight_grad,
        up_bias_grad,
        down_weight_grad,
        down_bias_grad,
    ) = (
        lax.psum(ln1_gain_grad.astype(jnp.bfloat16), ("grp", "ctx")).astype(jnp.float32),
        lax.psum(ln1_bias_grad.astype(jnp.bfloat16), ("grp", "ctx")).astype(jnp.float32),
        lax.psum(qkv_weight_grad.astype(jnp.bfloat16), ("grp", "ctx")).astype(jnp.float32),
        lax.psum(qv_bias_grad.astype(jnp.bfloat16), ("grp", "ctx")).astype(jnp.float32),
        lax.psum(out_weight_grad.astype(jnp.bfloat16), ("grp", "ctx")).astype(jnp.float32),
        lax.psum(out_bias_grad.astype(jnp.bfloat16), ("grp", "ctx")).astype(jnp.float32),
        lax.psum(ln2_gain_grad.astype(jnp.bfloat16), ("grp", "ctx")).astype(jnp.float32),
        lax.psum(ln2_bias_grad.astype(jnp.bfloat16), ("grp", "ctx")).astype(jnp.float32),
        lax.psum(up_weight_grad.astype(jnp.bfloat16), ("grp", "ctx")).astype(jnp.float32),
        lax.psum(up_bias_grad.astype(jnp.bfloat16), ("grp", "ctx")).astype(jnp.float32),
        lax.psum(down_weight_grad.astype(jnp.bfloat16), ("grp", "ctx")).astype(jnp.float32),
        lax.psum(down_bias_grad.astype(jnp.bfloat16), ("grp", "ctx")).astype(jnp.float32),
    )
    return (
        layer_output.reshape(1, row_count, width),
        input_grad.reshape(1, row_count, width),
        ln1_gain_grad,
        ln1_bias_grad,
        qkv_weight_grad,
        qv_bias_grad,
        out_weight_grad,
        out_bias_grad,
        ln2_gain_grad,
        ln2_bias_grad,
        up_weight_grad,
        up_bias_grad,
        down_weight_grad,
        down_bias_grad,
    )


def solution(mesh):
    placed = (
        P("grp", "ctx", None),
        P(),
        P(),
        P(None, None, "tp"),
        P(None, "tp"),
        P("tp", None),
        P(),
        P(),
        P(),
        P(None, "tp"),
        P("tp"),
        P("tp", None),
        P(),
        P("grp", "ctx", None),
        P(),
        P(),
        P(),
    )
    return jax.shard_map(
        per_device,
        mesh=mesh,
        in_specs=placed,
        out_specs=(
            P("grp", "ctx", None),
            P("grp", "ctx", None),
            P(),
            P(),
            P(None, None, "tp"),
            P(None, "tp"),
            P("tp", None),
            P(),
            P(),
            P(),
            P(None, "tp"),
            P("tp"),
            P("tp", None),
            P(),
        ),
        check_vma=False,
    )
```

profile of v0, /device:TPU:1, one launch (start us, length us, event | category | flops | bytes accessed | tf_op | source)
XLA Modules:
  0.0 1006.5 jit_solution(4476708514880778175)
XLA Ops:
  22.2 10.1 %all_gather.12 = bf16[2048,1,128]{2,0,1:T(8,128)(2,1)S(1)} all-gather(bf16[1024,1,128]{2,0,1:T(8,128)(2,1)S(1)} %fusion.86), channel_id=1, replica_groups=mesh['grp'=4,'tp'=16,'ctx'=2] {'ctx'}, dimensions={0}, use_global_device_ids=true | all-gather | bytes 786432 | tf_op jit(solution)/shard_map/all_gather | solution.py:104
  32.3 8.4 all-gather
  48.4 8.4 fusion.74
  57.5 145.0 %all-reduce.9.cloned.1.call-done = f32[1024,2048]{1,0:T(8,128)} async-done(((f32[1024,2048]{1,0:T(8,128)}), f32[1024,2048]{1,0:T(8,128)}) %all-reduce.9.cloned.1.call-update) | async-done | bytes 8388624 | tf_op jit(solution)/shard_map/psum | solution.py:118
  212.9 10.3 %convolution_convert_fusion.2 = bf16[1024,2048]{1,0:T(8,128)(2,1)} fusion(bf16[512,2048]{1,0:T(8,128)(2,1)} %param.28, bf16[2048,512]{1,0:T(8,128)(2,1)S(1)} %copy-done, f32[2048]{0:T(1024)S(1)} %convert_element_type.330, f32[2048]{0:T(1024)S(1)} %convert_element_type.329, f32[1024]{0:T(1024)S(1)} %add_rsqrt_fusion, f32[1024]{0:T(1024)S(1)} %broadcast_multiply_fusion.2, ...), kind=kOutput, calls=%fused_computation.63 | convolution fusion | flops 4319084544 | bytes 21006336 | tf_op jit(solution)/shard_map/dot_general | solution.py:133
  223.4 6.7 convert_bitcast_fusion
  230.1 96.1 %all-reduce.11.cloned.1.call-done = bf16[1024,2048]{1,0:T(8,128)(2,1)} async-done(((bf16[1024,2048]{1,0:T(8,128)(2,1)}), bf16[1024,2048]{1,0:T(8,128)(2,1)}) %all-reduce.11.cloned.1.call-update) | async-done | bytes 4194320 | tf_op jit(solution)/shard_map/psum | solution.py:135
  326.2 8.7 add_convert_fusion.2
  348.4 9.1 all_gather.14
  357.5 8.4 all-gather.1
  385.3 141.0 %all-reduce.13.cloned.1.call-done = f32[1024,2048]{1,0:T(8,128)} async-done(((f32[1024,2048]{1,0:T(8,128)}), f32[1024,2048]{1,0:T(8,128)}) %all-reduce.13.cloned.1.call-update) | async-done | bytes 8388624 | tf_op jit(solution)/shard_map/psum | solution.py:118
  526.4 9.9 fusion.138
  558.4 102.6 %all-reduce.15.cloned.1.call-done = bf16[1024,2048]{1,0:T(8,128)(2,1)} async-done(((bf16[1024,2048]{1,0:T(8,128)(2,1)}), bf16[1024,2048]{1,0:T(8,128)(2,1)}) %all-reduce.15.cloned.1.call-update) | async-done | bytes 4194320 | tf_op jit(solution)/shard_map/psum | solution.py:156
  666.8 6.5 fusion.6
  673.4 7.3 fusion.137
  700.6 7.6 fusion.34
  713.4 6.4 convolution_convert_fusion.3
  726.3 13.0 %reduce-scatter.5.cloned.1.call-done = bf16[1024,1,128]{0,2,1:T(8,128)(2,1)} async-done(((bf16[2048,1,128]{0,2,1:T(8,128)(2,1)}), bf16[1024,1,128]{0,2,1:T(8,128)(2,1)}) %reduce-scatter.5.cloned.1.call-update) | async-done | bytes 262160 | tf_op jit(solution)/shard_map/reduce_scatter | solution.py:189
  739.3 7.5 convolution_convert_fusion.4
  760.4 70.4 %all-reduce.19.cloned.1.call-done = (bf16[2048,3,128]{2,0,1:T(8,128)(2,1)}, bf16[128,2048]{1,0:T(8,128)(2,1)}, bf16[2048,512]{1,0:T(8,128)(2,1)}, bf16[512,2048]{1,0:T(8,128)(2,1)}) async-done(((bf16[2048,3,128]{2,0,1:T(8,128)(2,1)}, bf16[128,2048]{1,0:T(8,128)(2,1)}, bf16[2048,512]{1,0:T(8,128)(2,1)}, bf16[512,2048]{1,0:T(8,128)(2,1)}), (bf16[2048,3,128]{2,0,1:T(8,128)(2,1)}, bf16[128,2048]{1,0:T(8,128)(2,1)}, ...) | async-done | bytes 6291472 | tf_op jit(solution)/shard_map/psum | solution.py:232
  843.1 94.5 %all-reduce.17.cloned.1.call-done = bf16[1024,2048]{1,0:T(8,128)(2,1)} async-done(((bf16[1024,2048]{1,0:T(8,128)(2,1)}), bf16[1024,2048]{1,0:T(8,128)(2,1)}) %all-reduce.17.cloned.1.call-update) | async-done | bytes 4194320 | tf_op jit(solution)/shard_map/psum | solution.py:207
  946.1 6.5 fusion.7
  952.6 30.6 %all-reduce = (bf16[2048]{0:T(1024)(128)(2,1)S(1)}, bf16[2048]{0:T(1024)(128)(2,1)S(1)}, bf16[2,128]{1,0:T(2,128)(2,1)S(1)}, bf16[2048]{0:T(1024)(128)(2,1)S(1)}...) all-reduce(bf16[2048]{0:T(1024)(128)(2,1)S(1)} %get-tuple-element.1, ...), channel_id=1, replica_groups=mesh['grp'=4,'tp'=16,'ctx'=2] {'grp','ctx'}, use_global_device_ids=true, to_apply=%region_31.32 | all-reduce | flops 13056 | bytes 52224 | tf_op jit(solution)/shard_map/psum | solution.py:230
  988.0 11.3 %add_bitcast_fusion = f32[1,1024,2048]{2,1,0:T(8,128)} fusion(f32[1024,2048]{1,0:T(8,128)} %copy-done.4, f32[1024]{0:T(1024)S(1)} %negate_multiply_fusion, f32[1024]{0:T(1024)S(1)} %multiply_multiply_fusion.2, f32[1024,2048]{1,0:T(8,128)} %convert_bitcast_fusion, f32[1024]{0:T(1024)S(1)} %broadcast_multiply_fusion.1, f32[1024]{0:T(1024)S(1)} %fusion.117, ...), kind=kLoop, calls=%fused_computation.25 | loop fusion | flops 18874368 | bytes 29384704 | tf_op jit(solution)/shard_map/reshape | solution.py:245
  (186 shorter events, 164.8 us)
Async XLA Ops:
  7.2 205.7 %copy-start = (bf16[2048,512]{1,0:T(8,128)(2,1)S(1)}, bf16[2048,512]{1,0:T(8,128)(2,1)}, u32[]{:S(2)}) copy-start(bf16[2048,512]{1,0:T(8,128)(2,1)} %param.26) | copy-start | bytes 6291460
  7.2 195.2 %all-reduce.9.cloned.1.call-start = ((), (), s32[]{:S(2)}) async-start(), calls=%async_computation.2 | async-start | bytes 16777216 | tf_op jit(solution)/shard_map/psum | solution.py:118
  40.8 7.6 copy-start.14
  56.8 269.4 %all-reduce.11.cloned.1.call-start = ((), (), s32[]{:S(2)}) async-start(), calls=%async_computation.3 | async-start | bytes 8388608 | tf_op jit(solution)/shard_map/psum | solution.py:135
  202.5 8.2 copy-start.6
  212.9 10.4 %copy-start.27 = (bf16[2048]{0:T(1024)(128)(2,1)S(1)}, bf16[2048]{0:T(1024)(128)(2,1)}, u32[]{:S(2)}) copy-start(bf16[2048]{0:T(1024)(128)(2,1)} %param.29) | copy-start | bytes 12292
  223.3 303.0 %all-reduce.13.cloned.1.call-start = ((), (), s32[]{:S(2)}) async-start(), calls=%async_computation.4 | async-start | bytes 16777216 | tf_op jit(solution)/shard_map/psum | solution.py:118
  348.3 20.0 %copy-start.19 = (f32[1024,3,1,128]{3,0,1,2:T(8,128)}, f32[1024,3,1,128]{3,0,1,2:T(8,128)S(1)}, u32[]{:S(2)}) copy-start(f32[1024,3,1,128]{3,0,1,2:T(8,128)S(1)} %fusion.59) | copy-start | bytes 4718596
  382.7 278.3 %all-reduce.15.cloned.1.call-start = ((), (), s32[]{:S(2)}) async-start(), calls=%async_computation.5 | async-start | bytes 8388608 | tf_op jit(solution)/shard_map/psum | solution.py:156
  543.7 9.0 copy-start.12
  558.1 168.1 %reduce-scatter.3.cloned.1.call-start = ((), (), s32[]{:S(2)}) async-start(), calls=%async_computation.6 | async-start | bytes 786432 | tf_op jit(solution)/shard_map/reduce_scatter | solution.py:186
  661.0 12.3 %slice-start = ((s8[8388608]{0:T(1024)(128)(4,1)}), s8[4194304]{0:T(1024)(128)(4,1)S(1)}, s32[]{:S(2)}) async-start(s8[8388608]{0:T(1024)(128)(4,1)} %bitcast.168), calls=%async_computation.10 | async-start | bytes 8388608
  666.8 15.2 %slice-start.2 = ((s8[8388608]{0:T(1024)(128)(4,1)}), s8[4194304]{0:T(1024)(128)(4,1)S(1)}, s32[]{:S(2)}) async-start(s8[8388608]{0:T(1024)(128)(4,1)} %bitcast.170), calls=%async_computation.12 | async-start | bytes 8388608
  673.3 7.4 copy-start.15
  673.4 8.6 slice-start.3
  680.7 8.2 copy-start.4
  680.7 8.2 slice-start.4
  682.0 8.0 slice-start.5
  700.3 39.0 %reduce-scatter.5.cloned.1.call-start = ((), (), s32[]{:S(2)}) async-start(), calls=%async_computation.7 | async-start | bytes 786432 | tf_op jit(solution)/shard_map/reduce_scatter | solution.py:189
  713.3 117.5 %all-reduce.19.cloned.1.call-start = ((), (), s32[]{:S(2)}) async-start(), calls=%async_computation.9 | async-start | bytes 12582912 | tf_op jit(solution)/shard_map/psum | solution.py:232
  739.3 7.9 copy-start.20
  739.3 7.9 copy-start.21
  746.8 190.8 %all-reduce.17.cloned.1.call-start = ((), (), s32[]{:S(2)}) async-start(), calls=%async_computation.8 | async-start | bytes 8388608 | tf_op jit(solution)/shard_map/psum | solution.py:207
  830.8 9.7 copy-start.13
  (25 other events, 104.8 us)
Sparse Core Ops, SparseCore 0:
  56.9 145.5 all-reduce.8
  223.4 102.6 all-reduce.10
  382.8 143.5 all-reduce.12
  558.3 102.6 all-reduce.14
  700.4 18.4 reduce-scatter.2
  721.2 18.0 reduce-scatter.4
  747.0 83.7 all-reduce.18
  834.1 103.5 all-reduce.16
where the time goes:
time: 1010 us
  waiting for transfers between devices  663 us (66%)
  other arithmetic  141 us (14%)
  matrix products  97.4 us (10%)
  blocking collectives  66.7 us (7%)
  local copies, waits for them, and re-layouts  22 us (2%)
  between operations  15.3 us (2%)
    psum x2, waiting for transfers between devices, attend(): middle = rows_in + lax.psum(partial_out, 'tp') + out_bias_f  286 us
    psum x1, waiting for transfers between devices, per_device(): lax.psum(jnp.einsum('rf,df->rd', hidden_grad, up_weight, preferred_elemen...  103 us
    psum x1, waiting for transfers between devices, per_device(): lax.psum(partial_mlp.astype(jnp.bfloat16), 'tp').astype(jnp.float32)  96.1 us
    psum x1, waiting for transfers between devices, per_device(): lax.psum(jnp.einsum('rc,dc->rd', qkv_grad, qkv_flat, preferred_element_ty...  94.5 us
    psum x1, waiting for transfers between devices, per_device(): lax.psum(qkv_weight_grad.astype(jnp.bfloat16), ('grp', 'ctx'))  70.4 us
    psum x1, blocking collectives, per_device(): lax.psum(ln1_gain_grad.astype(jnp.bfloat16), ('grp', 'ctx'))  30.6 us
    reduce_sum x6, other arithmetic, layer_norm(): return centred * lax.rsqrt(variance + 1e-05) * gain_vec + bias_vec  29.9 us
    reduce_sum x4, other arithmetic, layer_norm(): average = jnp.mean(values, axis=-1, keepdims=True)  22.4 us
  transfers between devices with their start and end apart: 8, of which 7 were waited for; matrix products, arithmetic and copies ran while one was open for 6% of the time, Pallas kernels for 0%

commit v1 on v0

v1 whole, which is shorter than its diff:
```python
import math

import jax
import jax.numpy as jnp
from jax import lax
from jax.sharding import PartitionSpec as P

HD = 128
GROUPS = 3
EVERY = ("grp", "tp", "ctx")
N_GRP, N_TP, N_CTX, SIDE = 4, 16, 2, 4
fp32 = jnp.float32
bf16 = jnp.bfloat16


def device_id(grp, tx, tz, ctx):
    return (grp * N_TP + tx * SIDE + tz) * N_CTX + ctx


def line_groups(first_axis):
    groups = []
    for grp in range(N_GRP):
        for ctx in range(N_CTX):
            for fixed in range(SIDE):
                along_z = (grp % 2 == 0) == first_axis
                groups.append(
                    [
                        device_id(grp, fixed, i, ctx) if along_z else device_id(grp, i, fixed, ctx)
                        for i in range(SIDE)
                    ]
                )
    return groups


GROUPS_A = line_groups(True)
GROUPS_B = line_groups(False)


def swap_lines(groups, bit):
    return [(line[i], line[i ^ bit]) for line in groups for i in range(SIDE)]


def swap_all(grp_bit, ctx_bit):
    return [
        (device_id(g, x, z, c), device_id(g ^ grp_bit, x, z, c ^ ctx_bit))
        for g in range(N_GRP)
        for x in range(SIDE)
        for z in range(SIDE)
        for c in range(N_CTX)
    ]


def exchange(pieces, groups):
    return lax.all_to_all(pieces, EVERY, 0, 0, axis_index_groups=groups)


def spread(piece, groups):
    return exchange(jnp.broadcast_to(piece[None], (SIDE,) + piece.shape), groups)


def gather_lines(piece, groups):
    return lax.all_gather(piece, EVERY, axis=0, axis_index_groups=groups)


def layer_norm(values, gain_vec, bias_vec):
    average = jnp.mean(values, axis=-1, keepdims=True)
    centred = values - average
    variance = jnp.mean(centred * centred, axis=-1, keepdims=True)
    return centred * lax.rsqrt(variance + 1e-05) * gain_vec + bias_vec


def gelu_tanh(values):
    inner = math.sqrt(2.0 / math.pi) * (values + 0.044715 * values * values * values)
    return 0.5 * values * (1.0 + jnp.tanh(inner))


def token_places(block_order, layout_index, block_rows):
    slots = layout_index // block_rows
    column = jnp.arange(block_order.shape[0], dtype=jnp.int32)
    picked = jnp.sum(
        jnp.where(
            slots[:, None] == column[None, :],
            block_order[None, :],
            jnp.zeros_like(block_order)[None, :],
        ),
        axis=1,
    )
    return picked * block_rows + layout_index % block_rows


def position_shares(group_table, group_counts):
    member = (group_table[:, None] == jnp.arange(GROUPS, dtype=jnp.int32)[None, :]).astype(fp32)
    holders = jnp.sum(member, axis=0)
    counts_float = group_counts.astype(fp32)
    per_group = counts_float / (holders * jnp.sum(counts_float))
    return group_table.shape[0] * jnp.sum(member * per_group[None, :], axis=1)


def per_device(
    layer_input,
    ln1_gain,
    ln1_bias,
    qkv_weight,
    qv_bias,
    out_weight,
    out_bias,
    ln2_gain,
    ln2_bias,
    up_weight,
    up_bias,
    down_weight,
    down_bias,
    cotangent,
    group_table,
    group_counts,
    block_order,
):
    width = layer_input.shape[-1]
    rows = layer_input.shape[1]
    local = qkv_weight.shape[2]
    hidden_local = up_weight.shape[1]
    block_rows = rows // 2
    line_rows = rows // SIDE
    own_rows = line_rows // SIDE
    score_scale = 1.0 / math.sqrt(HD)
    grp_at = lax.axis_index("grp")
    tp_at = lax.axis_index("tp")
    ctx_at = lax.axis_index("ctx")
    even = grp_at % 2 == 0
    a_at = jnp.where(even, tp_at % SIDE, tp_at // SIDE)
    b_at = jnp.where(even, tp_at // SIDE, tp_at % SIDE)
    line_start = a_at * line_rows
    own_start = line_start + b_at * own_rows

    gain_one = ln1_gain.astype(fp32)
    bias_one = ln1_bias.astype(fp32)
    gain_two = ln2_gain.astype(fp32)
    bias_two = ln2_bias.astype(fp32)
    tokens = layer_input.reshape(rows, width)
    cot = cotangent.reshape(rows, width)
    own_tokens = lax.dynamic_slice_in_dim(tokens, own_start, own_rows, 0).astype(fp32)
    own_cot = lax.dynamic_slice_in_dim(cot, own_start, own_rows, 0).astype(fp32)
    qkv_flat = qkv_weight.reshape(width, 3 * local)

    out_lines = gather_lines(out_weight, GROUPS_A).reshape(SIDE * local, width)
    qkv_lines = gather_lines(qkv_flat, GROUPS_A)

    shares = position_shares(group_table, group_counts)
    grp_slots = jnp.arange(shares.shape[0], dtype=jnp.int32)
    my_share = jnp.sum(jnp.where(grp_slots == grp_at, shares, jnp.zeros_like(shares)))
    grad_out = cot.astype(fp32) * my_share
    grad_low = grad_out.astype(bf16)
    down_bias_grad = jnp.sum(grad_out, axis=0)

    index = jnp.arange(rows, dtype=jnp.int32)
    query_places = token_places(block_order, ctx_at * rows + index, block_rows)
    other_places = token_places(block_order, (1 - ctx_at) * rows + index, block_rows)
    key_places = jnp.concatenate([query_places, other_places])
    causal = query_places[:, None] >= key_places[None, :]
    normed = layer_norm(tokens.astype(fp32), gain_one, bias_one).astype(bf16)
    mixed = jnp.dot(normed, qkv_flat, preferred_element_type=fp32)
    query = (mixed[:, :local] + qv_bias[0].astype(fp32)).astype(bf16)
    key_own = mixed[:, local : 2 * local].astype(bf16)
    value_own = (mixed[:, 2 * local :] + qv_bias[1].astype(fp32)).astype(bf16)
    pair = jnp.stack([key_own, value_own])
    swap_ctx = [(0, 1), (1, 0)]
    pair_other = lax.ppermute(pair, "ctx", swap_ctx)
    keys = jnp.concatenate([key_own, pair_other[0]], axis=0)
    values = jnp.concatenate([value_own, pair_other[1]], axis=0)
    scores = jnp.einsum("qd,kd->qk", query, keys, preferred_element_type=fp32) * score_scale
    scores = jnp.where(causal, scores, -1e30)
    top_score = jnp.max(scores, axis=-1, keepdims=True)
    expo = jnp.exp(scores - top_score)
    probs = expo / jnp.sum(expo, axis=-1, keepdims=True)
    probs_low = probs.astype(bf16)
    heads = jnp.einsum("qk,kd->qd", probs_low, values, preferred_element_type=fp32).astype(bf16)

    heads_line = exchange(heads.reshape(SIDE, line_rows, local), GROUPS_A)
    heads_line = heads_line.transpose(1, 0, 2).reshape(line_rows, SIDE * local)
    partial_out = jnp.dot(heads_line, out_lines, preferred_element_type=fp32).astype(bf16)
    partial_out = exchange(partial_out.reshape(SIDE, own_rows, width), GROUPS_B)
    middle = own_tokens + jnp.sum(partial_out.astype(fp32), axis=0) + out_bias.astype(fp32)
    normed_two_own = layer_norm(middle, gain_two, bias_two).astype(bf16)
    normed_two = spread(normed_two_own, GROUPS_B).reshape(line_rows, width)
    normed_two = gather_lines(normed_two, GROUPS_A).reshape(rows, width)

    hidden = jnp.dot(normed_two, up_weight, preferred_element_type=fp32) + up_bias.astype(fp32)
    active, gelu_pull = jax.vjp(gelu_tanh, hidden)
    active = active.astype(bf16)
    active_grad = jnp.einsum("rd,fd->rf", grad_low, down_weight, preferred_element_type=fp32)
    hidden_grad = gelu_pull(active_grad)[0].astype(bf16)

    def sum_rows(partial):
        parts = exchange(partial.reshape(SIDE, line_rows, width), GROUPS_A)
        parts = jnp.sum(parts.astype(fp32), axis=0).astype(bf16)
        parts = exchange(parts.reshape(SIDE, own_rows, width), GROUPS_B)
        return jnp.sum(parts.astype(fp32), axis=0)

    normed_two_grad = sum_rows(
        jnp.einsum("rf,df->rd", hidden_grad, up_weight, preferred_element_type=fp32).astype(bf16)
    )
    norm_value, norm_pull = jax.vjp(layer_norm, middle, gain_two, bias_two)
    middle_part, ln2_gain_part, ln2_bias_part = norm_pull(normed_two_grad)
    middle_grad = own_cot * my_share + middle_part
    middle_low = spread(middle_grad.astype(bf16), GROUPS_B).reshape(line_rows, width)

    head_grad = jnp.einsum("rd,fd->rf", middle_low, out_lines, preferred_element_type=fp32)
    head_grad = head_grad.astype(bf16).reshape(line_rows, SIDE, local).transpose(1, 0, 2)
    head_grad = exchange(head_grad, GROUPS_A).reshape(rows, local)
    prob_grad = jnp.einsum("qd,kd->qk", head_grad, values, preferred_element_type=fp32)
    values_grad = jnp.einsum("qk,qd->kd", probs_low, head_grad, preferred_element_type=fp32)
    score_grad = (
        probs * (prob_grad - jnp.sum(probs * prob_grad, axis=-1, keepdims=True))
    ).astype(bf16)
    query_grad = (
        jnp.einsum("qk,kd->qd", score_grad, keys, preferred_element_type=fp32) * score_scale
    ).astype(bf16)
    keys_grad = (
        jnp.einsum("qk,qd->kd", score_grad, query, preferred_element_type=fp32) * score_scale
    )
    pair_grad = jnp.stack([keys_grad, values_grad])
    pair_from = lax.ppermute(pair_grad[:, rows:].astype(bf16), "ctx", swap_ctx)
    pair_grad = (pair_grad[:, :rows] + pair_from.astype(fp32)).astype(bf16)
    qkv_grad = jnp.concatenate([query_grad, pair_grad[0], pair_grad[1]], axis=1)

    qkv_grad_line = exchange(qkv_grad.reshape(SIDE, line_rows, 3 * local), GROUPS_A)
    normed_grad = jnp.einsum(
        "arc,adc->rd", qkv_grad_line, qkv_lines, preferred_element_type=fp32
    ).astype(bf16)
    normed_grad = exchange(normed_grad.reshape(SIDE, own_rows, width), GROUPS_B)
    normed_grad = jnp.sum(normed_grad.astype(fp32), axis=0)
    first_value, first_pull = jax.vjp(layer_norm, own_tokens, gain_one, bias_one)
    input_part, ln1_gain_part, ln1_bias_part = first_pull(normed_grad)
    input_grad_own = (middle_grad + input_part).astype(bf16)
    vector_part = jnp.concatenate(
        [
            jnp.stack(
                [
                    ln1_gain_part,
                    ln1_bias_part,
                    ln2_gain_part,
                    ln2_bias_part,
                    jnp.sum(middle_grad, axis=0),
                ]
            ),
            jnp.zeros((11, width), fp32),
        ]
    ).astype(bf16)
    final_line = spread(jnp.concatenate([input_grad_own, vector_part]), GROUPS_B)
    input_grad = spread(final_line[:, :own_rows].reshape(line_rows, width), GROUPS_A)
    input_grad = input_grad.reshape(1, rows, width).astype(fp32)
    vectors = jnp.sum(final_line[:, own_rows : own_rows + 8].astype(fp32), axis=0)
    for pairs in (
        swap_lines(GROUPS_A, 1),
        swap_lines(GROUPS_A, 2),
        swap_all(1, 0),
        swap_all(2, 0),
        swap_all(0, 1),
    ):
        vectors = vectors + lax.ppermute(vectors, EVERY, pairs)

    partial_mlp = jnp.dot(active, down_weight, preferred_element_type=fp32).astype(bf16)
    output_own = (middle + sum_rows(partial_mlp) + down_bias.astype(fp32)).astype(bf16)
    output_line = spread(output_own, GROUPS_B).reshape(line_rows, width)
    layer_output = spread(output_line, GROUPS_A).reshape(1, rows, width)

    def total(value):
        return lax.psum(value, ("grp", "ctx"))

    down_weight_grad = jnp.einsum("rf,rd->fd", active, grad_low, preferred_element_type=fp32)
    up_weight_grad = jnp.einsum("rd,rf->df", normed_two, hidden_grad, preferred_element_type=fp32)
    down_weight_grad, up_weight_grad = total(
        (down_weight_grad.astype(bf16), up_weight_grad.astype(bf16))
    )
    middle_rows = gather_lines(middle_low, GROUPS_A).reshape(rows, width)
    out_weight_grad = jnp.einsum("rf,rd->fd", heads, middle_rows, preferred_element_type=fp32)
    up_bias_grad = jnp.sum(hidden_grad.astype(fp32), axis=0)
    qv_bias_grad = jnp.concatenate(
        [
            jnp.sum(query_grad.astype(fp32), axis=0),
            jnp.sum(pair_grad[1].astype(fp32), axis=0),
        ]
    )
    small_rows = jnp.concatenate(
        [
            down_bias_grad[None],
            jnp.concatenate(
                [up_bias_grad, qv_bias_grad, jnp.zeros((width - hidden_local - 2 * local,), fp32)]
            )[None],
            jnp.zeros((14, width), fp32),
        ]
    )
    out_and_small = jnp.concatenate([out_weight_grad, small_rows], axis=0).astype(bf16)
    qkv_weight_grad = jnp.einsum("rd,rc->dc", normed, qkv_grad, preferred_element_type=fp32)
    out_and_small, qkv_weight_grad = total((out_and_small, qkv_weight_grad.astype(bf16)))
    out_weight_grad = out_and_small[:local].astype(fp32)
    small_rows = out_and_small[local : local + 2].astype(fp32)
    return (
        layer_output,
        input_grad,
        vectors[0],
        vectors[1],
        qkv_weight_grad.astype(fp32).reshape(width, 3, local),
        small_rows[1, hidden_local : hidden_local + 2 * local].reshape(2, local),
        out_weight_grad,
        vectors[4],
        vectors[2],
        vectors[3],
        up_weight_grad.astype(fp32),
        small_rows[1, :hidden_local],
        down_weight_grad.astype(fp32),
        small_rows[0],
    )


def solution(mesh):
    placed = (
        P("grp", "ctx", None),
        P(),
        P(),
        P(None, None, "tp"),
        P(None, "tp"),
        P("tp", None),
        P(),
        P(),
        P(),
        P(None, "tp"),
        P("tp"),
        P("tp", None),
        P(),
        P("grp", "ctx", None),
        P(),
        P(),
        P(),
    )
    return jax.shard_map(
        per_device,
        mesh=mesh,
        in_specs=placed,
        out_specs=(
            P("grp", "ctx", None),
            P("grp", "ctx", None),
            P(),
            P(),
            P(None, None, "tp"),
            P(None, "tp"),
            P("tp", None),
            P(),
            P(),
            P(),
            P(None, "tp"),
            P("tp"),
            P("tp", None),
            P(),
        ),
        check_vma=False,
    )
```

time: 1010 us -> 549 us (0.54)
  waiting for transfers between devices: 663 us -> 226 us
  starting transfers between devices: 1.64 us -> 79.2 us
  other arithmetic: 141 us -> 65.9 us
  matrix products: 97.4 us -> 66.3 us
    psum x6 -> x1, waiting for transfers between devices: 650 us -> 39.7 us  [total(): return lax.psum(value, ('grp', 'ctx'))]
    all_to_all x0 -> x10, waiting for transfers between devices: none -> 105 us  [exchange(): return lax.all_to_all(pieces, EVERY, 0, 0, axis_index_groups=groups)]
    all_to_all x0 -> x5, blocking collectives: none -> 57.7 us  [exchange(): return lax.all_to_all(pieces, EVERY, 0, 0, axis_index_groups=groups)]
    all_to_all x0 -> x10, starting transfers between devices: none -> 53.7 us  [exchange(): return lax.all_to_all(pieces, EVERY, 0, 0, axis_index_groups=groups)]
    ppermute x0 -> x7, waiting for transfers between devices: none -> 45.8 us  [the longest x5 30.4 us: per_device(): vectors = vectors + lax.ppermute(vectors, EVERY, pairs)]
    all_gather x4 -> x0, blocking collectives: 36.1 us -> none  [the longest x2 19.2 us: attend(): lax.all_gather(value_rows, 'ctx', axis=0, tiled=True)]
    all_gather x0 -> x4, waiting for transfers between devices: none -> 34.1 us  [gather_lines(): return lax.all_gather(piece, EVERY, axis=0, axis_index_groups=groups)]
    psum x1 -> x0, blocking collectives: 30.6 us -> none  [per_device(): lax.psum(ln1_gain_grad.astype(jnp.bfloat16), ('grp', 'ctx'))]
  transfers between devices with their start and end apart: 8 -> 22, of which waited for: 7 -> 18; matrix products, arithmetic and copies ran while one was open for 6% -> 22% of each run, Pallas kernels for 0% -> 0%
where the time goes in v1:
time: 549 us; the launch traced here: 539 us
  waiting for transfers between devices  226 us (41%)
  starting transfers between devices  79.2 us (14%)
  matrix products  66.3 us (12%)
  other arithmetic  65.9 us (12%)
  blocking collectives  57.7 us (11%)
  local copies, waits for them, and re-layouts  28.7 us (5%)
  between operations  15.2 us (3%)
    all_to_all x10, waiting for transfers between devices, exchange(): return lax.all_to_all(pieces, EVERY, 0, 0, axis_index_groups=groups)  105 us
    all_to_all x5, blocking collectives, exchange(): return lax.all_to_all(pieces, EVERY, 0, 0, axis_index_groups=groups)  57.7 us
    all_to_all x10, starting transfers between devices, exchange(): return lax.all_to_all(pieces, EVERY, 0, 0, axis_index_groups=groups)  53.7 us
    psum x1, waiting for transfers between devices, total(): return lax.psum(value, ('grp', 'ctx'))  39.7 us
    all_gather x4, waiting for transfers between devices, gather_lines(): return lax.all_gather(piece, EVERY, axis=0, axis_index_groups=groups)  34.1 us
    ppermute x5, waiting for transfers between devices, per_device(): vectors = vectors + lax.ppermute(vectors, EVERY, pairs)  30.4 us
    ppermute x5, starting transfers between devices, per_device(): vectors = vectors + lax.ppermute(vectors, EVERY, pairs)  18.8 us
    unnamed x108, local copies, waits for them, and re-layouts  13.9 us
  transfers between devices with their start and end apart: 22, of which 18 were waited for; matrix products, arithmetic and copies ran while one was open for 22% of the time, Pallas kernels for 0%

profile of v1, /device:TPU:1, one launch (start us, length us, event | category | flops | bytes accessed | tf_op | source)
XLA Modules:
  0.0 539.2 jit_solution(1832427905013151468)
XLA Ops:
  27.4 9.4 %collective-permute-done = bf16[2,1024,128]{2,1,0:T(8,128)(2,1)S(1)} collective-permute-done((bf16[2,1024,128]{2,1,0:T(8,128)(2,1)S(1)}, bf16[2,1024,128]{2,1,0:T(8,128)(2,1)S(1)}, u32[]{:S(2)}, u32[]{:S(2)}) %collective-permute-start) | collective-permute-done | bytes 524320 | tf_op jit(solution)/shard_map/ppermute | solution.py:167
  49.7 9.4 %all_to_all.75 = bf16[4,256,128]{2,1,0:T(8,128)(2,1)S(1)} all-to-all(bf16[4,256,128]{2,1,0:T(8,128)(2,1)S(1)} %bitcast.211), channel_id=1, replica_groups={{0,2,4,6},{8,10,12,14},{16,18,20,22},{24,26,28,30},{1,3,5,7},{9,11,13,1..., dimensions={0} | all-to-all | bytes 524288 | tf_op jit(solution)/shard_map/all_to_all | solution.py:54
  67.5 9.7 %all-to-all-done.1 = bf16[4,64,2048]{2,1,0:T(8,128)(2,1)S(1)} async-done(((bf16[4,64,2048]{2,1,0:T(8,128)(2,1)}), bf16[4,64,2048]{2,1,0:T(8,128)(2,1)S(1)}, u32[]{:S(2)}, u32[]{:S(2)}) %all-to-all-start.1) | async-done | bytes 1048608 | tf_op jit(solution)/shard_map/all_to_all | solution.py:54
  81.0 13.4 %all_to_all.76 = bf16[4,64,2048]{2,1,0:T(8,128)(2,1)} all-to-all(bf16[4,64,2048]{2,1,0:T(8,128)(2,1)S(1)} %broadcast_in_dim.76), channel_id=1, replica_groups={{0,8,16,24},{2,10,18,26},{4,12,20,28},{6,14,22,30},{1,9,17,25},{3,11,19..., dimensions={0} | all-to-all | bytes 2097152 | tf_op jit(solution)/shard_map/all_to_all | solution.py:54
  94.4 34.0 %all-gather.6.cloned.1.call-done = bf16[4,256,2048]{2,1,0:T(8,128)(2,1)} async-done(((bf16[1,256,2048]{2,1,0:T(8,128)(2,1)}), bf16[4,256,2048]{2,1,0:T(8,128)(2,1)}) %all-gather.6.cloned.1.call-update) | async-done | bytes 4194320 | tf_op jit(solution)/shard_map/all_gather | solution.py:62
  145.4 7.6 %fusion.127 = (bf16[512]{0:T(512)(128)(2,1)S(1)}, bf16[1024,512]{1,0:T(8,128)(2,1)S(1)}) fusion(f32[1024,512]{1,0:T(8,128)} %copy-done.45, f32[512]{0:T(512)S(1)} %convert_element_type.216, bf16[512,2048]{1,0:T(8,128)(2,1)S(1)} %copy-done, bf16[1,1024,2048]{2,1,0:T(8,128)(2,1)} %param.30, f32[]{:T(128)} %fusion.111), kind=kOutput, calls=%fused_computation.210 | convolution fusion | flops 2167406080 | bytes 9440260 | tf_op jit(solution)/shard_map/rd,fd->rf/dot_general | solution.py:190
  158.4 11.8 %all-to-all-done.3 = bf16[4,256,2048]{2,1,0:T(8,128)(2,1)} async-done(((bf16[4,256,2048]{2,1,0:T(8,128)(2,1)}), bf16[4,256,2048]{2,1,0:T(8,128)(2,1)}, u32[]{:S(2)}, u32[]{:S(2)}) %all-to-all-start.3) | async-done | bytes 4194336 | tf_op jit(solution)/shard_map/all_to_all | solution.py:54
  181.1 26.6 %all-to-all-done.7 = bf16[4,256,2048]{2,1,0:T(8,128)(2,1)} async-done(((bf16[4,256,2048]{2,1,0:T(8,128)(2,1)}), bf16[4,256,2048]{2,1,0:T(8,128)(2,1)}, u32[]{:S(2)}, u32[]{:S(2)}) %all-to-all-start.7) | async-done | bytes 4194336 | tf_op jit(solution)/shard_map/all_to_all | solution.py:54
  207.7 14.3 %all-to-all-start.4 = ((bf16[4,64,2048]{2,1,0:T(8,128)(2,1)}), bf16[4,64,2048]{2,1,0:T(8,128)(2,1)S(1)}, u32[]{:S(2)}, u32[]{:S(2)}) async-start(bf16[4,64,2048]{2,1,0:T(8,128)(2,1)} %bitcast.20), calls=%async_computation.4 | async-start | bytes 2097152 | tf_op jit(solution)/shard_map/all_to_all | solution.py:54
  226.3 9.1 %all-to-all-done.4 = bf16[4,64,2048]{2,1,0:T(8,128)(2,1)S(1)} async-done(((bf16[4,64,2048]{2,1,0:T(8,128)(2,1)}), bf16[4,64,2048]{2,1,0:T(8,128)(2,1)S(1)}, u32[]{:S(2)}, u32[]{:S(2)}) %all-to-all-start.4) | async-done | bytes 1048608 | tf_op jit(solution)/shard_map/all_to_all | solution.py:54
  239.9 8.7 %all-to-all-done.8 = bf16[4,64,2048]{2,1,0:T(8,128)(2,1)S(1)} async-done(((bf16[4,64,2048]{2,1,0:T(8,128)(2,1)}), bf16[4,64,2048]{2,1,0:T(8,128)(2,1)S(1)}, u32[]{:S(2)}, u32[]{:S(2)}) %all-to-all-start.8) | async-done | bytes 1048608 | tf_op jit(solution)/shard_map/all_to_all | solution.py:54
  253.2 12.5 %all_to_all.77 = bf16[4,64,2048]{2,1,0:T(8,128)(2,1)S(1)} all-to-all(bf16[4,64,2048]{2,1,0:T(8,128)(2,1)S(1)} %broadcast_in_dim.150), channel_id=1, replica_groups={{0,8,16,24},{2,10,18,26},{4,12,20,28},{6,14,22,30},{1,9,17,25},{3,11,19..., dimensions={0} | all-to-all | bytes 2097152 | tf_op jit(solution)/shard_map/all_to_all | solution.py:54
  266.6 8.9 %all_to_all.78 = bf16[4,256,128]{2,1,0:T(8,128)(2,1)S(1)} all-to-all(bf16[4,256,128]{2,1,0:T(8,128)(2,1)S(1)} %bitcast.217), channel_id=1, replica_groups={{0,2,4,6},{8,10,12,14},{16,18,20,22},{24,26,28,30},{1,3,5,7},{9,11,13,1..., dimensions={0} | all-to-all | bytes 524288 | tf_op jit(solution)/shard_map/all_to_all | solution.py:54
  294.4 6.0 %collective-permute-done.1 = bf16[2,1024,128]{2,1,0:T(8,128)(2,1)S(1)} collective-permute-done((bf16[2,1024,128]{2,1,0:T(8,128)(2,1)S(1)}, bf16[2,1024,128]{2,1,0:T(8,128)(2,1)S(1)}, u32[]{:S(2)}, u32[]{:S(2)}) %collective-permute-start.1) | collective-permute-done | bytes 524320 | tf_op jit(solution)/shard_map/ppermute | solution.py:222
  306.6 7.7 %all-to-all-done.11 = bf16[4,256,384]{2,1,0:T(8,128)(2,1)S(1)} async-done(((bf16[4,256,384]{2,1,0:T(8,128)(2,1)}), bf16[4,256,384]{2,1,0:T(8,128)(2,1)S(1)}, u32[]{:S(2)}, u32[]{:S(2)}) %all-to-all-start.11) | async-done | bytes 786464 | tf_op jit(solution)/shard_map/all_to_all | solution.py:54
  314.3 5.6 %fusion.42 = bf16[256,2048]{1,0:T(8,128)(2,1)} fusion(bf16[4,256,384]{2,1,0:T(8,128)(2,1)S(1)} %all-to-all-done.11, bf16[4,2048,384]{2,1,0:T(8,128)(2,1)} %all-gather.8.cloned.1.call-done), kind=kOutput, calls=%fused_computation.51 | convolution fusion | flops 1611137024 | bytes 8126464 | tf_op jit(solution)/shard_map/arc,adc->rd/dot_general | solution.py:227
  323.6 14.6 %all-to-all-done.12 = bf16[4,64,2048]{2,1,0:T(8,128)(2,1)S(1)} async-done(((bf16[4,64,2048]{2,1,0:T(8,128)(2,1)}), bf16[4,64,2048]{2,1,0:T(8,128)(2,1)S(1)}, u32[]{:S(2)}, u32[]{:S(2)}) %all-to-all-start.12) | async-done | bytes 1048608 | tf_op jit(solution)/shard_map/all_to_all | solution.py:54
  348.4 7.2 %all-to-all-done.5 = bf16[4,64,2048]{2,1,0:T(8,128)(2,1)S(1)} async-done(((bf16[4,64,2048]{2,1,0:T(8,128)(2,1)}), bf16[4,64,2048]{2,1,0:T(8,128)(2,1)S(1)}, u32[]{:S(2)}, u32[]{:S(2)}) %all-to-all-start.5) | async-done | bytes 1048608 | tf_op jit(solution)/shard_map/all_to_all | solution.py:54
  356.7 13.6 %all_to_all.79 = bf16[4,80,2048]{2,1,0:T(8,128)(2,1)S(1)} all-to-all(bf16[4,80,2048]{2,1,0:T(8,128)(2,1)S(1)} %broadcast_in_dim.154), channel_id=1, replica_groups={{0,8,16,24},{2,10,18,26},{4,12,20,28},{6,14,22,30},{1,9,17,25},{3,11,19..., dimensions={0} | all-to-all | bytes 2621440 | tf_op jit(solution)/shard_map/all_to_all | solution.py:54
  396.1 10.1 %all-to-all-done.6 = bf16[4,256,2048]{2,1,0:T(8,128)(2,1)} async-done(((bf16[4,256,2048]{2,1,0:T(8,128)(2,1)}), bf16[4,256,2048]{2,1,0:T(8,128)(2,1)}, u32[]{:S(2)}, u32[]{:S(2)}) %all-to-all-start.6) | async-done | bytes 4194336 | tf_op jit(solution)/shard_map/all_to_all | solution.py:54
  419.3 20.7 %collective-permute-done.2 = f32[8,2048]{1,0:T(8,128)S(1)} collective-permute-done((f32[8,2048]{1,0:T(8,128)S(1)}, f32[8,2048]{1,0:T(8,128)S(1)}, u32[]{:S(2)}, u32[]{:S(2)}) %collective-permute-start.2) | collective-permute-done | bytes 65568 | tf_op jit(solution)/shard_map/ppermute | solution.py:260
  445.1 10.9 %collective-permute-start.4 = (f32[8,2048]{1,0:T(8,128)S(1)}, f32[8,2048]{1,0:T(8,128)S(1)}, u32[]{:S(2)}, u32[]{:S(2)}) collective-permute-start(f32[8,2048]{1,0:T(8,128)S(1)} %add.285), channel_id=1, source_target_pairs={{0,32},{1,33},{2,34},{3,35},{4,36},{5,37},{6,38},{7,39},{8,40},{9,... | collective-permute-start | bytes 196616 | tf_op jit(solution)/shard_map/ppermute | solution.py:260
  467.7 6.7 %bitcast_convert_fusion = f32[1,1024,2048]{2,1,0:T(8,128)} fusion(bf16[1,1024,2048]{2,1,0:T(8,128)(2,1)} %bitcast.194), kind=kLoop, calls=%fused_computation.28 | loop fusion | flops 2097152 | bytes 12582912 | tf_op jit(solution)/shard_map/convert_element_type | solution.py:251
  474.4 39.7 %all-reduce.3.cloned.1.call-done = (bf16[2048,3,128]{2,0,1:T(8,128)(2,1)}, bf16[144,2048]{1,0:T(8,128)(2,1)}, bf16[2048,512]{1,0:T(8,128)(2,1)}, bf16[512,2048]{1,0:T(8,128)(2,1)}) async-done(((bf16[2048,3,128]{2,0,1:T(8,128)(2,1)}, bf16[144,2048]{1,0:T(8,128)(2,1)}, bf16[2048,512]{1,0:T(8,128)(2,1)}, bf16[512,2048]{1,0:T(8,128)(2,1)}), (bf16[2048,3,128]{2,0,1:T(8,128)(2,1)}, bf16[144,2048]{1,0:T(8,128)(2,1)}, ...) | async-done | bytes 6357008 | tf_op jit(solution)/shard_map/psum | solution.py:268
  (258 shorter events, 206.1 us)
Async XLA Ops:
  7.2 126.4 %copy-start = (bf16[512,2048]{1,0:T(8,128)(2,1)S(1)}, bf16[512,2048]{1,0:T(8,128)(2,1)}, u32[]{:S(2)}) copy-start(bf16[512,2048]{1,0:T(8,128)(2,1)} %param.28) | copy-start | bytes 6291460
  7.2 51.9 %all-gather.12.cloned.1.call-start = ((), (), s32[]{:S(2)}) async-start(), calls=%async_computation.18 | async-start | bytes 2621440 | tf_op jit(solution)/shard_map/all_gather | solution.py:62
  21.6 15.2 %collective-permute-start = (bf16[2,1024,128]{2,1,0:T(8,128)(2,1)S(1)}, bf16[2,1024,128]{2,1,0:T(8,128)(2,1)S(1)}, u32[]{:S(2)}, u32[]{:S(2)}) collective-permute-start(bf16[2,1024,128]{2,1,0:T(8,128)(2,1)S(1)} %pad_maximum_fusion.2), channel_id=1, source_target_pairs={{0,1},{1,0},{2,3},{3,2},{4,5},{5,4},{6,7},{7,6},{8,9},{9,8},{10,11... | collective-permute-start | bytes 1572872 | tf_op jit(solution)/shard_map/ppermute | solution.py:167
  62.4 14.8 %all-to-all-start.1 = ((bf16[4,64,2048]{2,1,0:T(8,128)(2,1)}), bf16[4,64,2048]{2,1,0:T(8,128)(2,1)S(1)}, u32[]{:S(2)}, u32[]{:S(2)}) async-start(bf16[4,64,2048]{2,1,0:T(8,128)(2,1)} %bitcast.208), calls=%async_computation.1 | async-start | bytes 2097152 | tf_op jit(solution)/shard_map/all_to_all | solution.py:54
  67.4 61.0 %all-gather.6.cloned.1.call-start = ((), (), s32[]{:S(2)}) async-start(), calls=%async_computation.15 | async-start | bytes 5242880 | tf_op jit(solution)/shard_map/all_gather | solution.py:62
  138.3 31.9 %all-to-all-start.3 = ((bf16[4,256,2048]{2,1,0:T(8,128)(2,1)}), bf16[4,256,2048]{2,1,0:T(8,128)(2,1)}, u32[]{:S(2)}, u32[]{:S(2)}) async-start(bf16[4,256,2048]{2,1,0:T(8,128)(2,1)} %bitcast.205), calls=%async_computation.3 | async-start | bytes 8388608 | tf_op jit(solution)/shard_map/all_to_all | solution.py:54
  170.2 37.5 %all-to-all-start.7 = ((bf16[4,256,2048]{2,1,0:T(8,128)(2,1)}), bf16[4,256,2048]{2,1,0:T(8,128)(2,1)}, u32[]{:S(2)}, u32[]{:S(2)}) async-start(bf16[4,256,2048]{2,1,0:T(8,128)(2,1)} %bitcast.204), calls=%async_computation.7 | async-start | bytes 8388608 | tf_op jit(solution)/shard_map/all_to_all | solution.py:54
  175.2 131.4 %all-gather.8.cloned.1.call-start = ((), (), s32[]{:S(2)}) async-start(), calls=%async_computation.16 | async-start | bytes 7864320 | tf_op jit(solution)/shard_map/all_gather | solution.py:62
  207.7 27.7 %all-to-all-start.4 = ((bf16[4,64,2048]{2,1,0:T(8,128)(2,1)}), bf16[4,64,2048]{2,1,0:T(8,128)(2,1)S(1)}, u32[]{:S(2)}, u32[]{:S(2)}) async-start(bf16[4,64,2048]{2,1,0:T(8,128)(2,1)} %bitcast.20), calls=%async_computation.4 | async-start | bytes 2097152 | tf_op jit(solution)/shard_map/all_to_all | solution.py:54
  235.4 13.2 %all-to-all-start.8 = ((bf16[4,64,2048]{2,1,0:T(8,128)(2,1)}), bf16[4,64,2048]{2,1,0:T(8,128)(2,1)S(1)}, u32[]{:S(2)}, u32[]{:S(2)}) async-start(bf16[4,64,2048]{2,1,0:T(8,128)(2,1)} %bitcast.210), calls=%async_computation.8 | async-start | bytes 2097152 | tf_op jit(solution)/shard_map/all_to_all | solution.py:54
  290.3 10.1 %collective-permute-start.1 = (bf16[2,1024,128]{2,1,0:T(8,128)(2,1)S(1)}, bf16[2,1024,128]{2,1,0:T(8,128)(2,1)S(1)}, u32[]{:S(2)}, u32[]{:S(2)}) collective-permute-start(bf16[2,1024,128]{2,1,0:T(8,128)(2,1)S(1)} %fusion.64), channel_id=1, source_target_pairs={{0,1},{1,0},{2,3},{3,2},{4,5},{5,4},{6,7},{7,6},{8,9},{9,8},{10,11... | collective-permute-start | bytes 1572872 | tf_op jit(solution)/shard_map/ppermute | solution.py:222
  302.5 11.8 %all-to-all-start.11 = ((bf16[4,256,384]{2,1,0:T(8,128)(2,1)}), bf16[4,256,384]{2,1,0:T(8,128)(2,1)S(1)}, u32[]{:S(2)}, u32[]{:S(2)}) async-start(bf16[4,256,384]{2,1,0:T(8,128)(2,1)} %pad_maximum_fusion.1), calls=%async_computation.11 | async-start | bytes 1572864 | tf_op jit(solution)/shard_map/all_to_all | solution.py:54
  306.0 107.9 %all-gather.10.cloned.1.call-start = ((), (), s32[]{:S(2)}) async-start(), calls=%async_computation.17 | async-start | bytes 5242880 | tf_op jit(solution)/shard_map/all_gather | solution.py:62
  306.6 31.6 %copy-start.25 = (bf16[64,2048]{1,0:T(8,128)(2,1)S(1)}, bf16[64,2048]{1,0:T(8,128)(2,1)}, u32[]{:S(2)}) copy-start(bf16[64,2048]{1,0:T(8,128)(2,1)} %get-tuple-element.31) | copy-start | bytes 786436
  319.9 18.3 %all-to-all-start.12 = ((bf16[4,64,2048]{2,1,0:T(8,128)(2,1)}), bf16[4,64,2048]{2,1,0:T(8,128)(2,1)S(1)}, u32[]{:S(2)}, u32[]{:S(2)}) async-start(bf16[4,64,2048]{2,1,0:T(8,128)(2,1)} %bitcast.216), calls=%async_computation.12 | async-start | bytes 2097152 | tf_op jit(solution)/shard_map/all_to_all | solution.py:54
  339.3 16.3 %all-to-all-start.5 = ((bf16[4,64,2048]{2,1,0:T(8,128)(2,1)}), bf16[4,64,2048]{2,1,0:T(8,128)(2,1)S(1)}, u32[]{:S(2)}, u32[]{:S(2)}) async-start(bf16[4,64,2048]{2,1,0:T(8,128)(2,1)} %broadcast_in_dim.142), calls=%async_computation.5 | async-start | bytes 2097152 | tf_op jit(solution)/shard_map/all_to_all | solution.py:54
  374.1 32.1 %all-to-all-start.6 = ((bf16[4,256,2048]{2,1,0:T(8,128)(2,1)}), bf16[4,256,2048]{2,1,0:T(8,128)(2,1)}, u32[]{:S(2)}, u32[]{:S(2)}) async-start(bf16[4,256,2048]{2,1,0:T(8,128)(2,1)} %broadcast_in_dim.144), calls=%async_computation.6 | async-start | bytes 8388608 | tf_op jit(solution)/shard_map/all_to_all | solution.py:54
  408.7 59.0 %all-to-all-start.14 = ((bf16[4,256,2048]{2,1,0:T(8,128)(2,1)}), bf16[4,256,2048]{2,1,0:T(8,128)(2,1)}, u32[]{:S(2)}, u32[]{:S(2)}) async-start(bf16[4,256,2048]{2,1,0:T(8,128)(2,1)} %broadcast_in_dim.156), calls=%async_computation.14 | async-start | bytes 8388608 | tf_op jit(solution)/shard_map/all_to_all | solution.py:54
  413.8 100.3 %all-reduce.3.cloned.1.call-start = ((), (), s32[]{:S(2)}) async-start(), calls=%async_computation.19 | async-start | bytes 12713984 | tf_op jit(solution)/shard_map/psum | solution.py:268
  417.9 22.1 %collective-permute-start.2 = (f32[8,2048]{1,0:T(8,128)S(1)}, f32[8,2048]{1,0:T(8,128)S(1)}, u32[]{:S(2)}, u32[]{:S(2)}) collective-permute-start(f32[8,2048]{1,0:T(8,128)S(1)} %convert_reduce_fusion.6), channel_id=1, source_target_pairs={{0,2},{2,0},{4,6},{6,4},{8,10},{10,8},{12,14},{14,12},{16,18},{18,... | collective-permute-start | bytes 196616 | tf_op jit(solution)/shard_map/ppermute | solution.py:260
  440.0 5.1 collective-permute-start.3
  445.1 11.8 %collective-permute-start.4 = (f32[8,2048]{1,0:T(8,128)S(1)}, f32[8,2048]{1,0:T(8,128)S(1)}, u32[]{:S(2)}, u32[]{:S(2)}) collective-permute-start(f32[8,2048]{1,0:T(8,128)S(1)} %add.285), channel_id=1, source_target_pairs={{0,32},{1,33},{2,34},{3,35},{4,36},{5,37},{6,38},{7,39},{8,40},{9,... | collective-permute-start | bytes 196616 | tf_op jit(solution)/shard_map/ppermute | solution.py:260
  456.8 4.8 collective-permute-start.5
  461.6 5.5 %collective-permute-start.6 = (f32[8,2048]{1,0:T(8,128)S(1)}, f32[8,2048]{1,0:T(8,128)S(1)}, u32[]{:S(2)}, u32[]{:S(2)}) collective-permute-start(f32[8,2048]{1,0:T(8,128)S(1)} %add.287), channel_id=1, source_target_pairs={{0,1},{1,0},{2,3},{3,2},{4,5},{5,4},{6,7},{7,6},{8,9},{9,8},{10,11... | collective-permute-start | bytes 196616 | tf_op jit(solution)/shard_map/ppermute | solution.py:260
  (51 other events, 440.2 us)
Sparse Core Ops, SparseCore 0:
  9.7 26.8 all-gather.11
  94.5 33.8 all-gather.5
  178.3 49.3 all-gather.7
  308.2 42.1 all-gather.9
  418.1 95.9 all-reduce.2
